TPU v7x, 32 devices: a whole 2x2x4 slice. The times are simulated.
32 devices in a mesh: dom: 8 (over y, x, core), tool: 4 (over z).
Axes of the slice: x: 2, y: 2, z: 4, core: 2. Of those that a mesh axis runs over, the one named last changes fastest.
Arguments:
- records: float32 [2048, 512], P(('dom', 'tool')), may hold values from -6 to 6
- tool_data: float32 [8192, 512], P(('dom', 'tool')), may hold values from -6 to 6
- owners: int32 [2048, 2], P(('dom', 'tool')), may hold values from 0 to 31, all different within a row; in each aligned block of 64 rows (0 to 63, 64 to 127, ...) at most 6 rows name the same one
- local_seg: int32 [2048, 2], P(('dom', 'tool')), may hold values from 0 to 255
- active: int32 [2048, 64], P(('dom', 'tool')), may hold values 0 or 1
- stiffness: float32 [2048, 5, 4096], P(('dom', 'tool')), may hold values from -0.3125 to 0.3125
- columns: int32 [2048, 5], P(('dom', 'tool')), may hold values from 0 to 67, as said below
- vectors: float32 [2048, 4096], P(('dom', 'tool')), may hold values from -6 to 6
Outputs:
- product: float32 [2048, 4096], P(('dom', 'tool'))
Inputs may be any that keep to these rules, and one draw needn't show every extreme that they name: Among the 64 node blocks of one device no owner is named by more than 6 candidates, a bound that some block reaches; a block's candidates name different owners. `columns`: the first column of each row is the row's own block, column 2 + b mod 64; the others lie within 2 blocks of it.
All inputs are finite; a program needn't handle non-finite values. No bound on the sum of `active` on one device may be relied on, other than what follows from the above.
Results may differ from a plain program's by a relative error of at most 0.0003.
Values sent between devices are 32-bit elements; how exact they have to be, the bound alone decides.
No kernel may reach another device: no remote copies, remote signals or barrier semaphores. Data moves between devices by JAX's collectives and lax.ppermute only.
A program may use at most 128 MiB of HBM per device.

v0:
```python
import functools
import math

import jax
import jax.numpy as jnp
from jax import lax
from jax.experimental import pallas as pl
from jax.experimental.pallas import tpu as pltpu
from jax.sharding import PartitionSpec as P

NODE = 64
NVEC = 64
FIELDS = 8
HB = 2
LANES = 128
SUB = 8
AXES = ("dom", "tool")
TURN = 1.0 / (2.0 * math.pi)
REACH = math.sqrt(math.log2(math.e) / 4.0)
SHARE = math.sqrt(0.05)
FAR = -1e30
SINE = (6.283164044071425, -41.33714233428813, 81.34076747811504, -70.99341826772617)
LIFT = math.log2(-SINE[3] * SHARE * 0.5)
F32 = jnp.float32
BF16 = jnp.bfloat16
VMEM = pl.BlockSpec(memory_space=pltpu.VMEM)
SMEM = pl.BlockSpec(memory_space=pltpu.SMEM)
HBM = pl.BlockSpec(memory_space=pltpu.HBM)
ROUND = 1.5 * 2.0**23
PARTS = 3


def params(mib):
    return pltpu.CompilerParams(vmem_limit_bytes=mib << 20)


def left_half(rows):
    return lax.broadcasted_iota(jnp.int32, (rows, LANES), 1) < NODE


def swap(x):
    return pltpu.roll(x, NODE, 1)


def split(x):
    high = x.astype(BF16)
    return high, (x - high.astype(F32)).astype(BF16)


def three(x):
    high = x.astype(BF16).astype(F32)
    rest = x - high
    mid = rest.astype(BF16).astype(F32)
    return high, mid, rest - mid


def fold(out, half):
    pairs = NODE // 2
    even, odd = out[:pairs], out[pairs:]
    return jnp.where(half, even, odd) + swap(jnp.where(half, odd, even))


def flip(tiles):
    tiles = list(tiles)
    row = lax.broadcasted_iota(jnp.int32, (SUB, LANES), 0)
    for d in (4, 2, 1):
        keep = (row & d) == 0
        for i in range(SUB):
            if i & d:
                continue
            a, b = tiles[i], tiles[i + d]
            if 2 * d == SUB:
                moved = pltpu.roll(jnp.where(keep, b, a), d, 0)
                tiles[i], tiles[i + d] = jnp.where(keep, a, moved), jnp.where(keep, moved, b)
            else:
                tiles[i] = jnp.where(keep, a, pltpu.roll(b, d, 0))
                tiles[i + d] = jnp.where(keep, pltpu.roll(a, SUB - d, 0), b)
    return tiles


def flip_all(tiles):
    runs = [flip(tiles[i : i + SUB]) for i in range(0, len(tiles), SUB)]
    return [jnp.concatenate([run[j] for run in runs], axis=0) for j in range(SUB)]


def tiles_from(blocks):
    out = []
    for at in range(0, blocks[0].shape[0], SUB):
        out += flip([x[at : at + SUB] for x in blocks])
    return out


def doubled(x, half):
    other = swap(x)
    return jnp.where(half, x, other), jnp.where(half, other, x)


def high_low(x, half):
    return jnp.where(half, x, x - x.astype(BF16).astype(F32))


def copies_of(sources, targets, sems):
    made = [pltpu.make_async_copy(a, b, sems.at[i]) for i, (a, b) in enumerate(zip(sources, targets))]
    for copy in made:
        copy.start()
    return made


def pair_fields(x, y):
    quarter = left_half(x.shape[0])
    return jnp.concatenate([jnp.where(quarter, x, swap(y)), jnp.where(quarter, swap(x), y)], axis=0)


def field_rows(shape):
    row = lax.broadcasted_iota(jnp.int32, shape, 0)
    place = (row < 2) | (row == 4)
    return row, place, (row != 7) & ~place


def ranks(hits):
    n = hits.shape[1]
    upper = (
        lax.broadcasted_iota(jnp.int32, (n, n), 0) <= lax.broadcasted_iota(jnp.int32, (n, n), 1)
    ).astype(BF16)
    return jnp.dot(hits.astype(F32).astype(BF16), upper, preferred_element_type=F32)


def prep_kernel(
    peers, segs, owners_hbm, seg_hbm, vec_hbm, send_ref, owners_ref, seg_ref, first_ref, last_ref, edge_ref, sems
):
    last = vec_hbm.shape[0] - 1
    got = copies_of(
        (owners_hbm, seg_hbm, vec_hbm.at[0], vec_hbm.at[last]), (owners_ref, seg_ref, first_ref, last_ref), sems
    )
    cands = owners_ref.shape[0]
    pairs = NODE // 2
    share = 2 * HB * pairs // peers
    got[0].wait()
    got[1].wait()
    wanted = [owners_ref[k : k + 1, :] * segs + seg_ref[k : k + 1, :] for k in range(cands)]
    wanted = jnp.concatenate(wanted, axis=1).astype(F32)
    send_ref[pl.ds(0, peers, stride=1 + share), :] = jnp.broadcast_to(wanted, (peers, LANES))
    got[2].wait()
    got[3].wait()
    for h in range(HB):
        edge_ref[h * pairs : (h + 1) * pairs, :] = first_ref[pl.ds(h, pairs, stride=SUB), :]
        edge_ref[(HB + h) * pairs : (HB + h + 1) * pairs, :] = last_ref[pl.ds(SUB - HB + h, pairs, stride=SUB), :]
    for r in range(share):
        send_ref[pl.ds(1 + r, peers, stride=1 + share), :] = edge_ref[pl.ds(r, peers, stride=share), :]


def rows_kernel(peers, capacity, stride, got_ref, part_ref, out_ref):
    segs, width = part_ref.shape[0], part_ref.shape[1] // PARTS
    chunks = width // LANES
    share = got_ref.shape[0] // peers - 1
    doms, tools = (lax.axis_size(axis) for axis in AXES)
    at_dom, at_tool = (lax.axis_index(axis) for axis in AXES)
    seg = lax.broadcasted_iota(jnp.int32, (peers, segs), 1).astype(F32)
    local = got_ref[pl.ds(0, peers, stride=1 + share), :] - ((at_dom * tools + at_tool) * segs).astype(F32)
    hits = (local >= 0.0) & (local < float(segs))
    rank = ranks(hits)
    picks = []
    for s in range(capacity):
        row = jnp.sum(jnp.where(hits & (rank == s + 1.0), local, 0.0), axis=1, keepdims=True)
        picks.append((seg == row).astype(F32).astype(BF16))
    picks = jnp.concatenate(picks, axis=0)
    for c in range(0, chunks, 2):
        got = None
        for p in range(PARTS):
            at = p * width + c * LANES
            term = jnp.dot(picks, part_ref[:, at : at + 2 * LANES], preferred_element_type=F32)
            got = term if got is None else got + term
        for s in range(capacity):
            for i in range(2):
                out_ref[pl.ds(s * chunks + c + i, peers, stride=stride * chunks), :] = got[
                    s * peers : (s + 1) * peers, i * LANES : (i + 1) * LANES
                ]
    me = at_tool * doms + at_dom
    peer = lax.broadcasted_iota(jnp.int32, (peers, LANES), 0)
    for r in range(share):
        edge = got_ref[pl.ds(1 + r, peers, stride=1 + share), :]
        following = jnp.where(
            peer < peers - doms, pltpu.roll(edge, peers - doms, 0), pltpu.roll(edge, peers - doms - 1, 0)
        )
        following = jnp.where(peer == peers - 1, 0.0, following)
        previous = jnp.where(peer >= doms, pltpu.roll(edge, doms, 0), pltpu.roll(edge, doms + 1, 0))
        previous = jnp.where(peer == 0, 0.0, previous)
        out_ref[pl.ds(capacity * chunks + r, peers, stride=stride * chunks), :] = jnp.where(
            me < peers // 2, following, previous
        )


def parts_kernel(after_prep, tool_hbm, part_ref, tool_ref, sems):
    copies_of((tool_hbm,), (tool_ref,), sems)[0].wait()
    width = tool_ref.shape[1]
    field = lax.broadcasted_iota(jnp.int32, tool_ref.shape, 1) // NODE
    scale = jnp.where(field < 3, REACH, jnp.where(field < 6, 3.0 * TURN, jnp.where(field == 6, TURN, 1.0)))
    for p, part in enumerate(three(tool_ref[...] * scale)):
        part_ref[:, p * width : (p + 1) * width] = part.astype(BF16)


def ordered(row, h, m, l, order):
    out = jnp.zeros(row.shape, F32)
    for value, name in ((h, "h"), (m, "m"), (l, "l")):
        for i, at in enumerate(order):
            if at == name:
                out = jnp.where(row == i, value, out)
    return out


def main_kernel(
    doms, peers, capacity, stride,
    columns_hbm, vec_hbm, rec_hbm, act_hbm, owners_hbm, stiff_hbm, out_hbm, slot_ref, own_ref, field_ref, edge_ref,
    columns_ref, vec_ref, rec_ref, act_ref, owners_ref, stiff_ref,
    wide_ref, left_ref, last_ref, out_ref, sems, out_sem,
):
    nnz, groups = stiff_ref.shape[:2]
    blocks = groups * SUB
    pairs = NODE // 2
    even_count = nnz // 2 * 2
    half = left_half(SUB)
    half_rows = left_half(pairs)
    got = copies_of(
        (columns_hbm, vec_hbm, rec_hbm, act_hbm, owners_hbm) + tuple(stiff_hbm.at[:, g] for g in range(groups)),
        (columns_ref, vec_ref, rec_ref, act_ref, owners_ref) + tuple(stiff_ref.at[:, g] for g in range(groups)),
        sems,
    )
    zero = jnp.zeros((NODE, LANES), BF16)
    for h in range(HB):
        wide_ref[h] = zero
        wide_ref[blocks + HB + h] = zero

    def tile(m):
        return pl.ds(m * SUB, SUB)

    def spread(g):
        for at in range(0, pairs, 2 * SUB):
            evens, odds = [], []
            for m in range(at, at + 2 * SUB):
                even, odd = doubled(vec_ref[g, tile(m), :], half)
                evens.append(high_low(even, half))
                odds.append(high_low(odd, half))
            for q, values in enumerate((evens, odds)):
                for j, x in enumerate(flip_all(values)):
                    own_ref[g * SUB + j, q * pairs + at : q * pairs + at + 2 * SUB, :] = x.astype(BF16)
            mixed = [x for both in zip(evens, odds) for x in both]
            for j, x in enumerate(flip_all(mixed)):
                wide_ref[HB + g * SUB + j, 2 * at : 2 * at + 4 * SUB, :] = x.astype(BF16)

    row, place, _ = field_rows((SUB, LANES))
    scale = jnp.where(place, REACH, 1.0)
    lane = lax.broadcasted_iota(jnp.int32, (SUB, LANES), 1)
    turn = lane // NODE * NODE + lane % pairs * 2 + lane % NODE // pairs

    def evens_first(x):
        return jnp.take_along_axis(x, turn, axis=1, mode="promise_in_bounds")

    def fields(g):
        for j in range(0, SUB, 2):
            x = rec_ref[g, pl.ds(j, FIELDS // 2, stride=SUB), :]
            y = rec_ref[g, pl.ds(j + 1, FIELDS // 2, stride=SUB), :]
            part = pair_fields(x, y) * scale
            norm = -0.5 * jnp.sum(jnp.where(place, part * part, 0.0), axis=0, keepdims=True)
            at = g * SUB + j
            flags = jnp.concatenate([act_ref[pl.ds(at, 1), :], act_ref[pl.ds(at + 1, 1), :]], axis=1)
            norm = jnp.where(flags == 0, FAR, norm)
            h, m, l = three(evens_first(part))
            norms = three(evens_first(jnp.broadcast_to(norm, (SUB, LANES))))
            slip = ordered(row, h[7:8], m[7:8], l[7:8], "hhmhlm")
            lists = [jnp.where(row == 7, n, v) for n, v in zip(norms + (1.0, 1.0, 1.0), (h, h, m, h, l, m))]
            more = jnp.zeros((LANES - 8 * SUB, LANES), F32)
            stack = jnp.concatenate(lists + [slip, swap(slip), more], axis=0).T.astype(BF16)
            field_ref[at] = stack[:NODE]
            field_ref[at + 1] = stack[NODE:]

    def prepare(g):
        for at in range(0, pairs, 2 * SUB):
            for e in range(0, nnz, 2):
                evens, odds = [], []
                for m in range(at, at + 2 * SUB):
                    x = stiff_ref[e, g, tile(m), :]
                    if e < even_count:
                        y = stiff_ref[e + 1, g, tile(m), :]
                        evens.append(jnp.where(half, x, swap(y)))
                        odds.append(jnp.where(half, swap(x), y))
                    else:
                        even, odd = doubled(x, half)
                        evens.append(high_low(even, half))
                        odds.append(high_low(odd, half))
                for q, values in enumerate((evens, odds)):
                    rows = slice(q * pairs + at, q * pairs + at + 2 * SUB)
                    for j, x in enumerate(flip_all(values)):
                        if e < even_count:
                            high, low = split(x)
                            cols = slice(e * NODE, (e + 2) * NODE)
                            left_ref[j, rows, cols] = high
                            left_ref[j, NODE + rows.start : NODE + rows.stop, cols] = low
                        else:
                            last_ref[j, rows, :] = x.astype(BF16)

    def product(g):
        folded = []
        for j in range(SUB):
            cols = [wide_ref[columns_ref[e, g * SUB + j]] for e in range(nnz)]
            folded.append(fold(times(left_ref[j], last_ref[j], cols), half_rows))
        for m, x in enumerate(tiles_from(folded)):
            out_ref[g, m * SUB : (m + 1) * SUB, :] = x

    def edges(side, g, first):
        for i in range(HB):
            j = first + i
            sums = []
            for h in range(HB):
                total = jnp.zeros((pairs, LANES), F32)
                for e in range(nnz):
                    here = columns_ref[e, g * SUB + j] == side * (blocks + HB) + h
                    total = total + jnp.where(here, stiff_ref[e, g, pl.ds(j, pairs, stride=SUB), :], 0.0)
                sums.append(total)
            x, y = sums
            left = jnp.concatenate([jnp.where(half_rows, x, swap(y)), jnp.where(half_rows, swap(x), y)], axis=0)
            high, low = split(left)
            edge_ref[side, i * 2 * NODE : i * 2 * NODE + NODE, :] = high
            edge_ref[side, i * 2 * NODE + NODE : (i + 1) * 2 * NODE, :] = low

    got[1].wait()
    spread(0)
    spread(1)
    got[5].wait()
    prepare(0)
    got[0].wait()
    edges(0, 0, 0)
    got[2].wait()
    got[3].wait()
    got[4].wait()
    cands = owners_ref.shape[0]
    owner_ids = lax.broadcasted_iota(jnp.int32, (peers, blocks), 0)
    before = jnp.zeros((peers, 1), F32)
    for k in range(cands):
        target = owners_ref[k : k + 1, :]
        hits = owner_ids == jnp.broadcast_to(target, (peers, blocks))
        places = jnp.where(hits, before + ranks(hits) - 1.0, 0.0)
        before = before + jnp.sum(hits.astype(F32), axis=1, keepdims=True)
        rank = jnp.sum(places, axis=0, keepdims=True)
        tools = peers // doms
        slot_ref[k : k + 1, :] = (target % tools * doms + target // tools) * stride + rank.astype(jnp.int32)

    def body(g, carry):
        pltpu.make_async_copy(stiff_hbm.at[:, g + 1], stiff_ref.at[:, g + 1], sems.at[6 + g]).wait()
        product(g)
        prepare(g + 1)
        spread(jnp.minimum(g + 2, groups - 1))
        fields(g)
        return carry

    lax.fori_loop(0, groups - 1, body, 0)
    product(groups - 1)
    inners = pltpu.make_async_copy(out_ref, out_hbm, out_sem)
    inners.start()
    fields(groups - 1)
    edges(1, groups - 1, SUB - HB)
    inners.wait()


def times(left, last, cols):
    even_count = left.shape[1] // NODE
    out = jnp.dot(left, jnp.concatenate(cols[:even_count], axis=0), preferred_element_type=F32)
    out = out[:NODE] + out[NODE:]
    if len(cols) > even_count:
        out = out + jnp.dot(last, jnp.concatenate([cols[-1], cols[-1]], axis=0), preferred_element_type=F32)
    return out


def contact_kernel(
    peers, capacity, stride, inner_hbm, slots_ref, rows_ref, field_ref, own_ref, edge_ref, out_hbm,
    slot_ref, inner_ref, out_ref, tall_ref, gram_ref, fold_ref, halo_ref, wide_ref, hold_ref, delta_ref, sems, out_sems,
):
    got = copies_of((slots_ref, inner_hbm), (slot_ref, inner_ref), sems)
    blocks = slot_ref.shape[1]
    groups = blocks // SUB
    pairs = NODE // 2
    half = left_half(pairs)
    full = left_half(NODE)
    row, place, angle = field_rows((SUB, LANES))
    none = jnp.zeros((SUB, LANES), F32)
    tail = row == 7

    def tile_of(reach, phase, slip):
        turn = jnp.abs(phase - ((phase + ROUND) - ROUND)) - 0.25
        square = turn * turn
        wave = square + SINE[2] / SINE[3]
        wave = wave * square + SINE[1] / SINE[3]
        wave = wave * square + SINE[0] / SINE[3]
        return jnp.exp2(reach) * (wave * turn) * (2.0 + jnp.tanh(slip))

    def tiles(g, j):
        raws, slips = [], []
        for i in range(2):
            b = g * SUB + j + i
            tool = pair_fields(rows_ref[slot_ref[0, b]], rows_ref[slot_ref[1, b]])
            norm = LIFT - 0.5 * jnp.sum(jnp.where(place, tool * tool, 0.0), axis=0, keepdims=True)
            h, m, l = three(tool)
            nh, nm, nl = three(norm)
            ones = jnp.where(tail, 1.0, 0.0)
            hp, mp, lp = (jnp.where(place, v, 0.0) for v in (h, m, l))
            ha, ma, la = (jnp.where(angle, v, 0.0) for v in (h, m, l))
            reach = [hp + ones, mp + ones, hp + ones, jnp.where(tail, nh, lp), jnp.where(tail, nm, hp), jnp.where(tail, nl, mp)]
            right = jnp.concatenate(
                [jnp.concatenate(x, axis=0).astype(BF16) for x in (reach, [ha, ma, ha, la, ha, ma])], axis=1
            )
            raws.append(jnp.dot(field_ref[b][:, : 6 * SUB], right, preferred_element_type=F32))
            slips.append(ordered(row, h[7:8], m[7:8], l[7:8], "hmhlhm"))
        right = jnp.concatenate(
            [jnp.concatenate([slips[0], none], axis=1), jnp.concatenate([none, slips[1]], axis=1)], axis=0
        ).astype(BF16)
        slide = jnp.dot(field_ref[g * SUB + j][:, 6 * SUB : 8 * SUB], right, preferred_element_type=F32)
        for i, raw in enumerate(raws):
            high, low = split(tile_of(raw[:, :LANES], raw[:, LANES:], slide[:, i * LANES : (i + 1) * LANES]))
            tall_ref[j + i, :NODE, :] = high
            tall_ref[j + i, NODE:, :] = low

    def gram(j):
        tall = tall_ref[j]
        out = lax.dot_general(tall, tall, (((1,), (1,)), ((), ())), preferred_element_type=F32)
        out = out[:NODE] + out[NODE:]
        gram_ref[j] = high_low(out + swap(out), full).astype(BF16)

    def apply(g, j):
        own = own_ref[g * SUB + j]
        out = jnp.dot(gram_ref[j], jnp.concatenate([own, own], axis=0), preferred_element_type=F32)
        fold_ref[j] = fold(out, half)

    def out_copy(g):
        return pltpu.make_async_copy(out_ref.at[g], out_hbm.at[g], out_sems.at[g])

    def emit(g):
        for m, x in enumerate(tiles_from([fold_ref[j] for j in range(SUB)])):
            spot = slice(m * SUB, (m + 1) * SUB)
            out_ref[g, spot, :] = inner_ref[g, spot, :] + x
        out_copy(g).start()

    def stages(g, first=0, last=3):
        if last >= 3:
            emit(g - 3)
        for j in range(0, SUB, 2):
            for i in range(j, j + 2):
                if first <= 2 <= last:
                    apply(g - 2, i)
                if first <= 1 <= last:
                    gram(i)
            if first == 0:
                tiles(g, j)

    share = 2 * HB * pairs // peers
    step = min(share, rows_ref.shape[1])
    for at in range(0, 2 * HB * pairs, step):
        q, r = at // share, at % share
        halo_ref[at : at + step, :] = rows_ref[q * stride + capacity + r // step][:step]
    got[0].wait()
    stages(0, last=0)
    for side in range(2):
        for h in range(HB):
            at = ((1 - side) * HB + h) * pairs
            even, odd = doubled(halo_ref[at : at + pairs, :], half)
            hold_ref[h, pl.ds(0, pairs, stride=2), :] = even
            hold_ref[h, pl.ds(1, pairs, stride=2), :] = odd
            wide_ref[side, h * NODE : (h + 1) * NODE, :] = high_low(hold_ref[h], full).astype(BF16)
        out = jnp.dot(edge_ref[side], wide_ref[side], preferred_element_type=F32)
        for i in range(HB):
            at = i * 2 * NODE
            delta_ref[side * HB + i] = fold(out[at : at + NODE] + out[at + NODE : at + 2 * NODE], half)
    stages(1, last=1)
    stages(2, last=2)
    got[1].wait()
    for i in range(2 * HB):
        g, j = (0, i) if i < HB else (groups - 1, SUB - 2 * HB + i)
        spot = pl.ds(j, pairs, stride=SUB)
        inner_ref[g, spot, :] = inner_ref[g, spot, :] + delta_ref[i]

    def body(g, carry):
        stages(g)
        return carry

    lax.fori_loop(3, groups, body, 0)
    for k in range(1, 4):
        stages(groups - 1 + k, first=k)
    for g in range(groups):
        out_copy(g).wait()


def per_device(records, tool_data, owners, local_seg, active, stiffness, columns, vectors):
    doms, tools = (lax.axis_size(axis) for axis in AXES)
    peers = doms * tools
    blocks, cands = owners.shape
    nnz = columns.shape[1]
    segs, width = tool_data.shape
    capacity = max(2, (3 * blocks * cands + 2 * peers - 1) // (2 * peers))
    groups = blocks // SUB
    pairs = NODE // 2
    chunks = width // LANES
    i32 = jnp.int32

    def shape(dims, dtype=F32):
        return jax.ShapeDtypeStruct(dims, dtype)

    def tiles_of(x, rows):
        lead = x.shape[:-2]
        n = len(lead)
        x = x.reshape(lead + (rows // SUB, SUB, x.shape[-1] // LANES, LANES))
        x = jnp.swapaxes(x, n + 1, n + 2)
        return x.reshape(lead + (rows // SUB, -1, LANES))

    vec = tiles_of(vectors, blocks)
    rec = tiles_of(records, blocks)
    stiff = tiles_of(jnp.swapaxes(stiffness, 0, 1), blocks)
    share = 2 * HB * pairs // peers
    stride = capacity + -(-share // chunks)

    def in_hbm(*arrays):
        return [pltpu.with_memory_space_constraint(x, pltpu.HBM) for x in arrays]

    send = pl.pallas_call(
        functools.partial(prep_kernel, peers, segs),
        out_shape=shape((peers * (1 + share), LANES)),
        in_specs=[HBM] * 3,
        out_specs=VMEM,
        scratch_shapes=[
            pltpu.VMEM((cands, blocks), i32),
            pltpu.VMEM((cands, blocks), i32),
            pltpu.VMEM(vec.shape[1:], F32),
            pltpu.VMEM(vec.shape[1:], F32),
            pltpu.VMEM((2 * HB * pairs, LANES), F32),
            pltpu.SemaphoreType.DMA((4,)),
        ],
        compiler_params=params(8),
        name="prep",
    )(*in_hbm(owners.T, local_seg.T, vec))

    members = AXES[::-1]
    wanted = lax.all_to_all(send.reshape(peers, 1 + share, 1, LANES), members, split_axis=0, concat_axis=0, tiled=True)
    wanted = wanted.reshape(peers * (1 + share), LANES)

    parts = pl.pallas_call(
        parts_kernel,
        out_shape=shape((segs, PARTS * width), BF16),
        in_specs=[HBM] * 2,
        out_specs=VMEM,
        scratch_shapes=[pltpu.VMEM(tool_data.shape, F32), pltpu.SemaphoreType.DMA((1,))],
        compiler_params=params(8),
        cost_estimate=pl.CostEstimate(flops=1 << 20, bytes_accessed=4 << 20, transcendentals=0),
        name="parts",
    )(*in_hbm(send, tool_data))

    rows_out = pl.pallas_call(
        functools.partial(rows_kernel, peers, capacity, stride),
        out_shape=shape((peers * stride * chunks, LANES)),
        in_specs=[VMEM] * 2,
        out_specs=VMEM,
        compiler_params=params(8),
        name="rows",
    )(wanted, parts)
    fetched = lax.all_to_all(
        rows_out.reshape(peers, stride, chunks, LANES), members, split_axis=0, concat_axis=0, tiled=True
    )

    wide = (blocks, NODE, LANES)
    left = (2 * NODE, nnz // 2 * 2 * NODE)
    inner, slot, own, fields, edges = pl.pallas_call(
        functools.partial(main_kernel, doms, peers, capacity, stride),
        out_shape=(
            pltpu.HBM(vec.shape, F32),
            shape((cands, blocks), i32),
            shape(wide, BF16),
            shape(wide, BF16),
            shape((2, HB * 2 * NODE, LANES), BF16),
        ),
        in_specs=[HBM] * 6,
        out_specs=(HBM,) + (VMEM,) * 4,
        scratch_shapes=[
            pltpu.SMEM((nnz, blocks), i32),
            pltpu.VMEM(vec.shape, F32),
            pltpu.VMEM(rec.shape, F32),
            pltpu.VMEM(active.shape, i32),
            pltpu.VMEM((cands, blocks), i32),
            pltpu.VMEM(stiff.shape, F32),
            pltpu.VMEM((blocks + 2 * HB, NODE, LANES), BF16),
            pltpu.VMEM((SUB,) + left, BF16),
            pltpu.VMEM((SUB, NODE, LANES), BF16),
            pltpu.VMEM(vec.shape, F32),
            pltpu.SemaphoreType.DMA((groups + 5,)),
            pltpu.SemaphoreType.DMA,
        ],
        compiler_params=params(20),
        cost_estimate=pl.CostEstimate(
            flops=6 * blocks * nnz * NODE * NODE * NVEC, bytes_accessed=24 << 20, transcendentals=0
        ),
        name="main",
    )(*in_hbm(columns.T, vec, rec, active, owners.T, stiff))

    out = pl.pallas_call(
        functools.partial(contact_kernel, peers, capacity, stride),
        out_shape=pltpu.HBM(vec.shape, F32),
        in_specs=[HBM] + [VMEM] * 5,
        out_specs=HBM,
        scratch_shapes=[
            pltpu.SMEM((cands, blocks), i32),
            pltpu.VMEM(vec.shape, F32),
            pltpu.VMEM(vec.shape, F32),
            pltpu.VMEM((SUB, 2 * NODE, LANES), BF16),
            pltpu.VMEM((SUB, NODE, LANES), BF16),
            pltpu.VMEM((SUB, pairs, LANES), F32),
            pltpu.VMEM((2 * HB * pairs, LANES), F32),
            pltpu.VMEM((2, HB * NODE, LANES), BF16),
            pltpu.VMEM((HB, NODE, LANES), F32),
            pltpu.VMEM((2 * HB, pairs, LANES), F32),
            pltpu.SemaphoreType.DMA((2,)),
            pltpu.SemaphoreType.DMA((groups,)),
        ],
        compiler_params=params(16),
        cost_estimate=pl.CostEstimate(
            flops=80 * blocks * cands * NODE * NODE, bytes_accessed=4 << 20, transcendentals=2 * blocks * cands * NODE * NODE
        ),
        name="contact",
    )(*in_hbm(inner), slot, fetched.reshape(peers * stride, chunks, LANES), fields, own, edges)
    out = out.reshape(groups, pairs, SUB, LANES)
    return jnp.swapaxes(out, 1, 2).reshape(blocks, NODE * NVEC)


def solution(mesh):
    split_rows = P(AXES, None)
    return jax.shard_map(
        per_device,
        mesh=mesh,
        in_specs=(split_rows,) * 5 + (P(AXES, None, None),) + (split_rows,) * 2,
        out_specs=split_rows,
        check_vma=False,
    )
```

profile of v0, /device:TPU:0, one launch (start us, length us, event | category | flops | bytes accessed | tf_op | source)
XLA Modules:
  0.0 40.9 jit_solution(1728635361399281559)
XLA Ops:
  0.0 1.7 %prep.1.after_prep = f32[160,128]{1,0:T(8,128)} custom-call(s32[2,64]{1,0:T(2,128)} %bitcast.36, s32[2,64]{1,0:T(2,128)} %bitcast.38, f32[8,256,128]{2,1,0:T(8,128)} %bitcast.32), custom_call_target="tpu_custom_call" | custom-call | tf_op jit(solution)/shard_map/prep/pallas_call | solution.py:521
  1.7 7.3 %all-to-all-start = ((f32[32,5,1,128]{3,2,1,0:T(1,128)}), f32[32,5,1,128]{3,2,1,0:T(1,128)S(1)}, u32[]{:S(2)}, u32[]{:S(2)}) async-start(f32[32,5,1,128]{3,2,1,0:T(1,128)} %bitcast.15), calls=%async_computation | async-start | bytes 163840 | tf_op jit(solution)/shard_map/all_to_all | solution.py:539
  9.0 1.2 %parts.1.part_ref = bf16[256,1536]{1,0:T(8,128)(2,1)S(1)} custom-call(f32[160,128]{1,0:T(8,128)} %prep.1.after_prep, f32[256,512]{1,0:T(8,128)} %tool_hbm.1), custom_call_target="tpu_custom_call" | custom-call | flops 1048576 | bytes 4194304 | tf_op jit(solution)/shard_map/parts/pallas_call | solution.py:542
  10.2 6.4 %all-to-all-done = f32[32,5,1,128]{3,2,1,0:T(1,128)S(1)} async-done(((f32[32,5,1,128]{3,2,1,0:T(1,128)}), f32[32,5,1,128]{3,2,1,0:T(1,128)S(1)}, u32[]{:S(2)}, u32[]{:S(2)}) %all-to-all-start) | async-done | bytes 81952 | tf_op jit(solution)/shard_map/all_to_all | solution.py:539
  16.6 1.3 %rows.1 = f32[896,128]{1,0:T(8,128)} custom-call(f32[160,128]{1,0:T(8,128)S(1)} %bitcast.30, bf16[256,1536]{1,0:T(8,128)(2,1)S(1)} %parts.1.part_ref), custom_call_target="tpu_custom_call" | custom-call | tf_op jit(solution)/shard_map/rows/pallas_call | solution.py:553
  17.9 2.6 %all-to-all-start.1 = ((f32[32,7,4,128]{3,2,1,0:T(4,128)}), f32[32,7,4,128]{3,2,1,0:T(4,128)S(1)}, u32[]{:S(2)}, u32[]{:S(2)}) async-start(f32[32,7,4,128]{3,2,1,0:T(4,128)} %bitcast.17), calls=%async_computation.1 | async-start | bytes 917504 | tf_op jit(solution)/shard_map/all_to_all | solution.py:561
  20.5 11.3 %main.1 = (f32[8,256,128]{2,1,0:T(8,128)}, s32[2,64]{1,0:T(2,128)S(1)}, bf16[64,64,128]{2,1,0:T(8,128)(2,1)S(1)}, bf16[64,64,128]{2,1,0:T(8,128)(2,1)S(1)}, bf16[2,256,128]{2,1,0:T(8,128)(2,1)S(1)}) custom-call(s32[5,64]{1,0:T(8,128)} %bitcast.35, f32[8,256,128]{2,1,0:T(8,128)} %bitcast.33, f32[8,32,128]{2,1,0:T(8,128)} %bitcast.34, s32[64,64]{1,0:T(8,128)} %act_hbm.1, ...), custom_call_target="tpu_custom_call" | custom-call | flops 503316480 | bytes 25165824 | tf_op jit(solution)/shard_map/main/pallas_call | solution.py:567
  31.8 3.1 %all-to-all-done.1 = f32[32,7,4,128]{3,2,1,0:T(4,128)S(1)} async-done(((f32[32,7,4,128]{3,2,1,0:T(4,128)}), f32[32,7,4,128]{3,2,1,0:T(4,128)S(1)}, u32[]{:S(2)}, u32[]{:S(2)}) %all-to-all-start.1) | async-done | bytes 458784 | tf_op jit(solution)/shard_map/all_to_all | solution.py:561
  34.9 6.1 %contact.1 = f32[8,256,128]{2,1,0:T(8,128)} custom-call(f32[8,256,128]{2,1,0:T(8,128)} %get-tuple-element.10.inner_hbm, s32[2,64]{1,0:T(2,128)S(1)} %get-tuple-element.11.slots_ref, f32[224,4,128]{2,1,0:T(4,128)S(1)} %bitcast.29, bf16[64,64,128]{2,1,0:T(8,128)(2,1)S(1)} %get-tuple-element.12.field_ref, bf16[64,64,128]{2,1,0:T(8,128)(2,1)S(1)} %get-tuple-element.13.own_ref, ...), custom_call_target="tpu_custom_call" | custom-call | flops 41943040 | bytes 4194304 | tf_op jit(solution)/shard_map/contact/pallas_call | solution.py:599
Async XLA Ops:
  1.7 14.9 %all-to-all-start = ((f32[32,5,1,128]{3,2,1,0:T(1,128)}), f32[32,5,1,128]{3,2,1,0:T(1,128)S(1)}, u32[]{:S(2)}, u32[]{:S(2)}) async-start(f32[32,5,1,128]{3,2,1,0:T(1,128)} %bitcast.15), calls=%async_computation | async-start | bytes 163840 | tf_op jit(solution)/shard_map/all_to_all | solution.py:539
  17.9 17.0 %all-to-all-start.1 = ((f32[32,7,4,128]{3,2,1,0:T(4,128)}), f32[32,7,4,128]{3,2,1,0:T(4,128)S(1)}, u32[]{:S(2)}, u32[]{:S(2)}) async-start(f32[32,7,4,128]{3,2,1,0:T(4,128)} %bitcast.17), calls=%async_computation.1 | async-start | bytes 917504 | tf_op jit(solution)/shard_map/all_to_all | solution.py:561
where the time goes:
time: 41.2 us; the launch traced here: 40.9 us
  Pallas kernels  21.5 us (52%)
  starting transfers between devices  9.9 us (24%)
  waiting for transfers between devices  9.45 us (23%)
    pallas_call x1, Pallas kernels, per_device(): pl.pallas_call(functools.partial(main_kernel, doms, peers, capacity, stri...  11.3 us
    all_to_all x1, starting transfers between devices, per_device(): lax.all_to_all(send.reshape(peers, 1 + share, 1, LANES), members, split_a...  7.3 us
    all_to_all x1, waiting for transfers between devices, per_device(): lax.all_to_all(send.reshape(peers, 1 + share, 1, LANES), members, split_a...  6.38 us
    pallas_call x1, Pallas kernels, per_device(): pl.pallas_call(functools.partial(contact_kernel, peers, capacity, stride)...  6.07 us
    all_to_all x1, waiting for transfers between devices, per_device(): lax.all_to_all(rows_out.reshape(peers, stride, chunks, LANES), members, s...  3.07 us
    all_to_all x1, starting transfers between devices, per_device(): lax.all_to_all(rows_out.reshape(peers, stride, chunks, LANES), members, s...  2.6 us
    pallas_call x1, Pallas kernels, per_device(): pl.pallas_call(functools.partial(prep_kernel, peers, segs), out_shape=sha...  1.69 us
    pallas_call x1, Pallas kernels, per_device(): pl.pallas_call(functools.partial(rows_kernel, peers, capacity, stride), o...  1.29 us
  transfers between devices with their start and end apart: 2, of which 2 were waited for; matrix products, arithmetic and copies ran while one was open for 0% of the time, Pallas kernels for 31%

commit v1 on v0

--- a/solution.py
+++ b/solution.py
@@ -442,11 +442,12 @@
         if last >= 3:
             emit(g - 3)
         for j in range(0, SUB, 2):
-            for i in range(j, j + 2):
-                if first <= 2 <= last:
-                    apply(g - 2, i)
-                if first <= 1 <= last:
-                    gram(i)
+            if first <= 2 <= last:
+                apply(g - 2, j)
+                apply(g - 2, j + 1)
+            if first <= 1 <= last:
+                gram(j)
+                gram(j + 1)
             if first == 0:
                 tiles(g, j)
 

time: 41.2 us -> 41.4 us (level)
  transfers between devices with their start and end apart: 2 -> 2, of which waited for: 2 -> 2; matrix products, arithmetic and copies ran while one was open for 0% -> 0% of each run, Pallas kernels for 31% -> 30%
where the time goes in v1:
time: 41.4 us; the launch traced here: 41.1 us
  Pallas kernels  21.8 us (53%)
  starting transfers between devices  9.9 us (24%)
  waiting for transfers between devices  9.45 us (23%)
    pallas_call x1, Pallas kernels, per_device(): pl.pallas_call(functools.partial(main_kernel, doms, peers, capacity, stri...  11.3 us
    all_to_all x1, starting transfers between devices, per_device(): lax.all_to_all(send.reshape(peers, 1 + share, 1, LANES), members, split_a...  7.3 us
    all_to_all x1, waiting for transfers between devices, per_device(): lax.all_to_all(send.reshape(peers, 1 + share, 1, LANES), members, split_a...  6.38 us
    pallas_call x1, Pallas kernels, per_device(): pl.pallas_call(functools.partial(contact_kernel, peers, capacity, stride)...  6.28 us
    all_to_all x1, waiting for transfers between devices, per_device(): lax.all_to_all(rows_out.reshape(peers, stride, chunks, LANES), members, s...  3.07 us
    all_to_all x1, starting transfers between devices, per_device(): lax.all_to_all(rows_out.reshape(peers, stride, chunks, LANES), members, s...  2.6 us
    pallas_call x1, Pallas kernels, per_device(): pl.pallas_call(functools.partial(prep_kernel, peers, segs), out_shape=sha...  1.69 us
    pallas_call x1, Pallas kernels, per_device(): pl.pallas_call(functools.partial(rows_kernel, peers, capacity, stride), o...  1.29 us
  transfers between devices with their start and end apart: 2, of which 2 were waited for; matrix products, arithmetic and copies ran while one was open for 0% of the time, Pallas kernels for 30%

profile of v1, /device:TPU:0, one launch (start us, length us, event | category | flops | bytes accessed | tf_op | source)
XLA Modules:
  0.0 41.1 jit_solution(7145429401041139153)
XLA Ops:
  0.0 1.7 %prep.1.after_prep = f32[160,128]{1,0:T(8,128)} custom-call(s32[2,64]{1,0:T(2,128)} %bitcast.36, s32[2,64]{1,0:T(2,128)} %bitcast.38, f32[8,256,128]{2,1,0:T(8,128)} %bitcast.32), custom_call_target="tpu_custom_call" | custom-call | tf_op jit(solution)/shard_map/prep/pallas_call | solution.py:522
  1.7 7.3 %all-to-all-start = ((f32[32,5,1,128]{3,2,1,0:T(1,128)}), f32[32,5,1,128]{3,2,1,0:T(1,128)S(1)}, u32[]{:S(2)}, u32[]{:S(2)}) async-start(f32[32,5,1,128]{3,2,1,0:T(1,128)} %bitcast.15), calls=%async_computation | async-start | bytes 163840 | tf_op jit(solution)/shard_map/all_to_all | solution.py:540
  9.0 1.2 %parts.1.part_ref = bf16[256,1536]{1,0:T(8,128)(2,1)S(1)} custom-call(f32[160,128]{1,0:T(8,128)} %prep.1.after_prep, f32[256,512]{1,0:T(8,128)} %tool_hbm.1), custom_call_target="tpu_custom_call" | custom-call | flops 1048576 | bytes 4194304 | tf_op jit(solution)/shard_map/parts/pallas_call | solution.py:543
  10.2 6.4 %all-to-all-done = f32[32,5,1,128]{3,2,1,0:T(1,128)S(1)} async-done(((f32[32,5,1,128]{3,2,1,0:T(1,128)}), f32[32,5,1,128]{3,2,1,0:T(1,128)S(1)}, u32[]{:S(2)}, u32[]{:S(2)}) %all-to-all-start) | async-done | bytes 81952 | tf_op jit(solution)/shard_map/all_to_all | solution.py:540
  16.6 1.3 %rows.1 = f32[896,128]{1,0:T(8,128)} custom-call(f32[160,128]{1,0:T(8,128)S(1)} %bitcast.30, bf16[256,1536]{1,0:T(8,128)(2,1)S(1)} %parts.1.part_ref), custom_call_target="tpu_custom_call" | custom-call | tf_op jit(solution)/shard_map/rows/pallas_call | solution.py:554
  17.9 2.6 %all-to-all-start.1 = ((f32[32,7,4,128]{3,2,1,0:T(4,128)}), f32[32,7,4,128]{3,2,1,0:T(4,128)S(1)}, u32[]{:S(2)}, u32[]{:S(2)}) async-start(f32[32,7,4,128]{3,2,1,0:T(4,128)} %bitcast.17), calls=%async_computation.1 | async-start | bytes 917504 | tf_op jit(solution)/shard_map/all_to_all | solution.py:562
  20.5 11.3 %main.1 = (f32[8,256,128]{2,1,0:T(8,128)}, s32[2,64]{1,0:T(2,128)S(1)}, bf16[64,64,128]{2,1,0:T(8,128)(2,1)S(1)}, bf16[64,64,128]{2,1,0:T(8,128)(2,1)S(1)}, bf16[2,256,128]{2,1,0:T(8,128)(2,1)S(1)}) custom-call(s32[5,64]{1,0:T(8,128)} %bitcast.35, f32[8,256,128]{2,1,0:T(8,128)} %bitcast.33, f32[8,32,128]{2,1,0:T(8,128)} %bitcast.34, s32[64,64]{1,0:T(8,128)} %act_hbm.1, ...), custom_call_target="tpu_custom_call" | custom-call | flops 503316480 | bytes 25165824 | tf_op jit(solution)/shard_map/main/pallas_call | solution.py:568
  31.8 3.1 %all-to-all-done.1 = f32[32,7,4,128]{3,2,1,0:T(4,128)S(1)} async-done(((f32[32,7,4,128]{3,2,1,0:T(4,128)}), f32[32,7,4,128]{3,2,1,0:T(4,128)S(1)}, u32[]{:S(2)}, u32[]{:S(2)}) %all-to-all-start.1) | async-done | bytes 458784 | tf_op jit(solution)/shard_map/all_to_all | solution.py:562
  34.9 6.3 %contact.1 = f32[8,256,128]{2,1,0:T(8,128)} custom-call(f32[8,256,128]{2,1,0:T(8,128)} %get-tuple-element.10.inner_hbm, s32[2,64]{1,0:T(2,128)S(1)} %get-tuple-element.11.slots_ref, f32[224,4,128]{2,1,0:T(4,128)S(1)} %bitcast.29, bf16[64,64,128]{2,1,0:T(8,128)(2,1)S(1)} %get-tuple-element.12.field_ref, bf16[64,64,128]{2,1,0:T(8,128)(2,1)S(1)} %get-tuple-element.13.own_ref, ...), custom_call_target="tpu_custom_call" | custom-call | flops 41943040 | bytes 4194304 | tf_op jit(solution)/shard_map/contact/pallas_call | solution.py:600
Async XLA Ops:
  1.7 14.9 %all-to-all-start = ((f32[32,5,1,128]{3,2,1,0:T(1,128)}), f32[32,5,1,128]{3,2,1,0:T(1,128)S(1)}, u32[]{:S(2)}, u32[]{:S(2)}) async-start(f32[32,5,1,128]{3,2,1,0:T(1,128)} %bitcast.15), calls=%async_computation | async-start | bytes 163840 | tf_op jit(solution)/shard_map/all_to_all | solution.py:540
  17.9 17.0 %all-to-all-start.1 = ((f32[32,7,4,128]{3,2,1,0:T(4,128)}), f32[32,7,4,128]{3,2,1,0:T(4,128)S(1)}, u32[]{:S(2)}, u32[]{:S(2)}) async-start(f32[32,7,4,128]{3,2,1,0:T(4,128)} %bitcast.17), calls=%async_computation.1 | async-start | bytes 917504 | tf_op jit(solution)/shard_map/all_to_all | solution.py:562
